TPU v7x, 32 devices: a whole 2x2x4 slice. The times are simulated.
32 devices in a mesh: seq: 8 (over y, x, core), dp: 4 (over z).
Axes of the slice: x: 2, y: 2, z: 4, core: 2. Of those that a mesh axis runs over, the one named last changes fastest.
Arguments:
- queries: bfloat16 [4, 4096, 1024], P('dp', 'seq'), may hold values from -6 to 6
- key_rows: bfloat16 [4, 4096, 1024], P('dp', 'seq'), may hold values from -6 to 6
- value_rows: bfloat16 [4, 4096, 1024], P('dp', 'seq'), may hold values from -6 to 6
- gate_rows: bfloat16 [4, 4096, 1024], P('dp', 'seq'), may hold values from -6 to 6
- cotangent: bfloat16 [4, 4096, 1024], P('dp', 'seq'), may hold values from -6 to 6
- far_blocks: int32 [4, 32, 4], P('dp'), may hold values from 0 to 31, as said below
- treated: int32 [4, 32], P('dp'), may hold values 0 or 1
- norm_gain: float32 [1024], replicated, may hold values from 0.1 to 1.9
- out_weight: bfloat16 [1024, 1024], replicated, may hold values from -0.1875 to 0.1875
Outputs:
- output: bfloat16 [4, 4096, 1024], P('dp', 'seq')
- grad_queries: bfloat16 [4, 4096, 1024], P('dp', 'seq')
- grad_keys: bfloat16 [4, 4096, 1024], P('dp', 'seq')
- grad_values: bfloat16 [4, 4096, 1024], P('dp', 'seq')
- grad_gate: bfloat16 [4, 4096, 1024], P('dp', 'seq')
- grad_weight: float32 [1024, 1024], P(('seq', 'dp'))
- grad_gain: float32 [1024], replicated
Inputs may be any that keep to these rules, and one draw needn't show every extreme that they name: `far_blocks`: every entry names a block of the same history that is held by another index of seq than its query block. Of the 16 entries of the query blocks held by index s of seq, 3 name blocks of index (s + o) mod 8 for o = 1 and o = 2, and 2 for each other o from 3 to 7; which entries these are, and which block of that index, are drawn.
All inputs are finite; a program needn't handle non-finite values. No bound on the sum of `treated` on one device may be relied on, other than what follows from the above.
Results may differ from a plain program's by a relative error of at most 0.0065.
Values may be sent and summed in bfloat16 or wider, within the bound.
A program may use at most 192 MiB of HBM per device.

v0:
```python
import jax
import jax.numpy as jnp
from jax import lax
from jax.sharding import PartitionSpec as P

HEADS = 8
HEAD_DIM = 128
BLK = 128
FAR = 4
epsilon = 1e-05


def from_behind(value, axis, by):
    peers = lax.axis_size(axis)
    pairs = [(i, i + by) for i in range(peers) if 0 <= i + by < peers]
    return lax.ppermute(value, axis, pairs)


def to_heads(rows):
    return rows.reshape(rows.shape[:-1] + (HEADS, rows.shape[-1] // HEADS))


def as_bf16(values):
    return values.astype(jnp.bfloat16)


def pair_scores(query_part, key_part):
    scores = jnp.einsum(
        "pqhd,pkhd->phqk",
        to_heads(query_part),
        to_heads(key_part),
        preferred_element_type=jnp.float32,
    )
    return scores * HEAD_DIM ** (-0.5)


def pair_forward(query_part, key_part, value_part, pair_mask):
    weights = as_bf16(jax.nn.silu(pair_scores(query_part, key_part)) * pair_mask[:, None])
    result = jnp.einsum(
        "phqk,pkhd->pqhd", weights, to_heads(value_part), preferred_element_type=jnp.float32
    )
    return result.reshape(query_part.shape)


def pair_backward(query_part, key_part, value_part, grad_part, pair_mask):
    scores = pair_scores(query_part, key_part)
    logistic = jax.nn.sigmoid(scores)
    weights = as_bf16(jax.nn.silu(scores) * pair_mask[:, None])
    grad_heads = to_heads(grad_part)
    grad_weights = jnp.einsum(
        "pqhd,pkhd->phqk", grad_heads, to_heads(value_part), preferred_element_type=jnp.float32
    )
    grad_value = jnp.einsum(
        "phqk,pqhd->pkhd", weights, grad_heads, preferred_element_type=jnp.float32
    )
    grad_scores = as_bf16(
        grad_weights
        * logistic
        * (1.0 + scores * (1.0 - logistic))
        * pair_mask[:, None]
        * HEAD_DIM ** (-0.5)
    )
    grad_query = jnp.einsum(
        "phqk,pkhd->pqhd", grad_scores, to_heads(key_part), preferred_element_type=jnp.float32
    )
    grad_key = jnp.einsum(
        "phqk,pqhd->pkhd", grad_scores, to_heads(query_part), preferred_element_type=jnp.float32
    )
    row_shape = query_part.shape
    return (
        grad_query.reshape(row_shape),
        grad_key.reshape(row_shape),
        grad_value.reshape(row_shape),
    )


def far_plan(far_all, my_index, seq_count, blocks, capacity):
    block_ids = far_all.reshape(seq_count, blocks * FAR)
    owners = block_ids // blocks
    local_ids = block_ids % blocks
    positions = jnp.arange(blocks * FAR)
    same_owner = owners[:, :, None] == owners[:, None, :]
    before = positions[None, :] < positions[:, None]
    slot_rank = jnp.sum(same_owner & before[None], axis=2)
    slot_ids = jnp.arange(capacity)
    send_hit = (owners[:, None, :] == my_index) & (slot_rank[:, None, :] == slot_ids[None, :, None])
    all_local = jnp.sum(jnp.where(send_hit, local_ids[:, None, :], 0), axis=2).reshape(-1)
    all_ok = jnp.any(send_hit, axis=2).reshape(-1)
    my_owners = lax.dynamic_index_in_dim(owners, my_index, 0, keepdims=False)
    my_ranks = lax.dynamic_index_in_dim(slot_rank, my_index, 0, keepdims=False)
    slot_count = seq_count * capacity
    read_at = my_owners * capacity + my_ranks
    back_hit = read_at[None, :] == jnp.arange(slot_count)[:, None]
    return (all_local, all_ok, read_at, back_hit)


def body(
    queries, key_rows, value_rows, gate_rows, cotangent, far_blocks, treated, norm_gain, out_weight
):
    width = queries.shape[2]
    blocks = queries.shape[1] // BLK
    seq_count = lax.axis_size("seq")
    my_index = lax.axis_index("seq")
    requests = blocks * FAR
    capacity = (requests + seq_count - 2) // (seq_count - 1)
    slot_count = seq_count * capacity
    query_blocks = queries[0].reshape(blocks, BLK, width)
    key_blocks = key_rows[0].reshape(blocks, BLK, width)
    value_blocks = value_rows[0].reshape(blocks, BLK, width)
    both_blocks = jnp.concatenate([key_blocks, value_blocks], axis=2)
    from_prev = from_behind(both_blocks[blocks - 1], "seq", 1)
    prev_both = jnp.concatenate([from_prev[None], both_blocks[:-1]], axis=0)
    prev_keys = prev_both[:, :, :width]
    prev_values = prev_both[:, :, width:]
    causal = jnp.tril(jnp.ones((BLK, BLK), jnp.float32))[None]
    all_ones = jnp.ones((1, BLK, BLK), jnp.float32)
    all_local, all_ok, read_at, back_hit = far_plan(
        far_blocks[0], my_index, seq_count, blocks, capacity
    )
    block_ids = lax.dynamic_slice_in_dim(far_blocks[0], my_index * blocks, blocks, 0).reshape(
        requests
    )
    far_mask = treated[0][block_ids].astype(jnp.float32)[:, None, None]
    far_queries = jnp.repeat(query_blocks, FAR, axis=0)
    back_matrix = back_hit.astype(jnp.bfloat16)
    local_onehot = ((all_local[None, :] == jnp.arange(blocks)[:, None]) & all_ok[None, :]).astype(
        jnp.bfloat16
    )
    diag_out = pair_forward(query_blocks, key_blocks, value_blocks, causal)
    prev_out = pair_forward(query_blocks, prev_keys, prev_values, all_ones)
    send_both = jnp.where(
        all_ok[:, None, None], both_blocks[all_local], jnp.zeros((), jnp.bfloat16)
    )
    got_both = lax.all_to_all(
        send_both.reshape(seq_count, capacity, BLK, 2 * width),
        "seq",
        split_axis=0,
        concat_axis=0,
        tiled=True,
    )
    received = got_both.reshape(slot_count, BLK, 2 * width)
    far_both = received[read_at]
    far_keys = far_both[:, :, :width]
    far_values = far_both[:, :, width:]
    far_terms = as_bf16(pair_forward(far_queries, far_keys, far_values, far_mask))
    far_sum = (
        lax.optimization_barrier(far_terms)
        .astype(jnp.float32)
        .reshape(blocks, FAR, BLK, width)
        .sum(axis=1)
    )
    attention = (diag_out + prev_out + far_sum).reshape(blocks * BLK, width)
    centered = attention - jnp.mean(attention, axis=1, keepdims=True)
    inv_std = lax.rsqrt(jnp.mean(centered * centered, axis=1, keepdims=True) + epsilon)
    normed = centered * inv_std
    gate_vals = gate_rows[0].astype(jnp.float32)
    mixed = as_bf16(normed * norm_gain * gate_vals)
    output = jnp.dot(mixed, out_weight, preferred_element_type=jnp.float32).astype(jnp.bfloat16)
    grad_in = cotangent[0]
    grad_mixed = lax.dot_general(
        grad_in, out_weight, (((1,), (1,)), ((), ())), preferred_element_type=jnp.float32
    )
    grad_weight = lax.psum_scatter(
        lax.dot_general(
            mixed, grad_in, (((0,), (0,)), ((), ())), preferred_element_type=jnp.float32
        ),
        ("seq", "dp"),
        scatter_dimension=0,
        tiled=True,
    )
    grad_gate = as_bf16(grad_mixed * normed * norm_gain)
    scaled = grad_mixed * gate_vals
    grad_gain = lax.psum(jnp.sum(scaled * normed, axis=0), ("seq", "dp"))
    grad_hat = scaled * norm_gain
    grad_attn = inv_std * (
        grad_hat
        - jnp.mean(grad_hat, axis=1, keepdims=True)
        - normed * jnp.mean(grad_hat * normed, axis=1, keepdims=True)
    )
    grad_blocks = as_bf16(grad_attn).reshape(blocks, BLK, width)
    dq_diag, dk_diag, dv_diag = pair_backward(
        query_blocks, key_blocks, value_blocks, grad_blocks, causal
    )
    dq_prev, dk_prev, dv_prev = pair_backward(
        query_blocks, prev_keys, prev_values, grad_blocks, all_ones
    )
    prev_terms = lax.optimization_barrier(as_bf16(jnp.concatenate([dk_prev, dv_prev], axis=2)))
    from_next = from_behind(prev_terms[0], "seq", -1)
    next_terms = jnp.concatenate([prev_terms[1:], from_next[None]], axis=0).astype(jnp.float32)
    far_grads = jnp.repeat(grad_blocks, FAR, axis=0)
    dq_far, dk_far, dv_far = pair_backward(far_queries, far_keys, far_values, far_grads, far_mask)
    query_terms = as_bf16(dq_far)
    back_terms = as_bf16(jnp.concatenate([dk_far, dv_far], axis=2))
    send_back = jnp.dot(
        back_matrix, back_terms.reshape(requests, -1), preferred_element_type=jnp.float32
    )
    send_back = as_bf16(send_back).reshape(slot_count, BLK, 2 * width)
    got_back = lax.all_to_all(
        send_back.reshape(seq_count, capacity, BLK, 2 * width),
        "seq",
        split_axis=0,
        concat_axis=0,
        tiled=True,
    )
    owned_terms = got_back.reshape(slot_count, BLK * 2 * width)
    far_query = (
        lax.optimization_barrier(query_terms)
        .astype(jnp.float32)
        .reshape(blocks, FAR, BLK, width)
        .sum(axis=1)
    )
    owned_sum = jnp.dot(
        local_onehot, lax.optimization_barrier(owned_terms), preferred_element_type=jnp.float32
    )
    owned_sum = owned_sum.reshape(blocks, BLK, 2 * width)
    rows = blocks * BLK
    grad_queries = as_bf16(dq_diag + dq_prev + far_query).reshape(1, rows, width)
    key_total = jnp.concatenate([dk_diag, dv_diag], axis=2) + next_terms + owned_sum
    grad_keys = as_bf16(key_total[:, :, :width]).reshape(1, rows, width)
    grad_values = as_bf16(key_total[:, :, width:]).reshape(1, rows, width)
    return (
        output[None],
        grad_queries,
        grad_keys,
        grad_values,
        grad_gate[None],
        grad_weight,
        grad_gain,
    )


def solution(mesh):
    in_specs = (
        P("dp", "seq", None),
        P("dp", "seq", None),
        P("dp", "seq", None),
        P("dp", "seq", None),
        P("dp", "seq", None),
        P("dp", None, None),
        P("dp", None),
        P(),
        P(),
    )
    out_specs = (
        P("dp", "seq", None),
        P("dp", "seq", None),
        P("dp", "seq", None),
        P("dp", "seq", None),
        P("dp", "seq", None),
        P(("seq", "dp"), None),
        P(),
    )
    return jax.shard_map(body, mesh=mesh, in_specs=in_specs, out_specs=out_specs, check_vma=False)
```

profile of v0, /device:TPU:0, one launch (start us, length us, event | category | flops | bytes accessed | tf_op | source)
XLA Modules:
  0.0 594.2 jit_solution(34854243904092478)
XLA Ops:
  12.2 7.5 %gather_fusion = bf16[24,128,2048]{2,1,0:T(8,128)(2,1)} fusion(bf16[4,128,2048]{2,1,0:T(8,128)(2,1)} %pad_maximum_fusion.1, s32[1024]{0:T(1024)S(1)} %pad_clamp_fusion.2), kind=kCustom, calls=%fused_computation | custom fusion | bytes 25165920 | tf_op jit(solution)/shard_map/gather | solution.py:132
  19.7 10.6 %broadcast_select_fusion = bf16[8,3,128,2048]{3,2,1,0:T(8,128)(2,1)} fusion(bf16[8,3,128,2048]{3,2,1,0:T(8,128)(2,1)} %bitcast.251, pred[8,3]{1,0:T(8,128)(4,1)S(1)} %copy.282), kind=kLoop, calls=%fused_computation.4 | loop fusion | flops 6291456 | bytes 25165848 | tf_op jit(solution)/shard_map/jit(_where)/select_n | solution.py:131
  30.3 5.5 all-to-all-start
  73.0 102.6 %all-to-all-done = bf16[8,3,128,2048]{3,2,1,0:T(8,128)(2,1)} async-done(((bf16[8,3,128,2048]{3,2,1,0:T(8,128)(2,1)}), bf16[8,3,128,2048]{3,2,1,0:T(8,128)(2,1)}, u32[]{:S(2)}, u32[]{:S(2)}) %all-to-all-start) | async-done | bytes 12582944 | tf_op jit(solution)/shard_map/all_to_all | solution.py:134
  175.6 9.5 %gather_fusion.1 = bf16[16,128,2048]{2,1,0:T(8,128)(2,1)} fusion(bf16[24,128,2048]{2,1,0:T(8,128)(2,1)} %bitcast.11, s32[1024]{0:T(1024)S(1)} %pad_clamp_fusion.1), kind=kCustom, calls=%fused_computation.1 | custom fusion | bytes 16777280 | tf_op jit(solution)/shard_map/gather | solution.py:142
  185.1 6.1 %fusion.73 = (bf16[16,128,1024]{2,1,0:T(8,128)(2,1)}, bf16[16,128,1024]{2,1,0:T(8,128)(2,1)}) fusion(bf16[16,128,2048]{2,1,0:T(8,128)(2,1)} %gather_fusion.1), kind=kLoop, calls=%fused_computation.143 | loop fusion | bytes 16777216 | tf_op jit(solution)/shard_map/slice | solution.py:143
  191.1 6.4 %copy.285 = bf16[16,128,1024]{1,2,0:T(8,128)(2,1)} copy(bf16[16,128,1024]{2,1,0:T(8,128)(2,1)} %get-tuple-element.18) | data formatting | bytes 8388608 | tf_op jit(solution)/shard_map/slice | solution.py:143
  197.6 6.3 %copy.284 = bf16[16,128,1024]{1,2,0:T(8,128)(2,1)} copy(bf16[16,128,1024]{2,1,0:T(8,128)(2,1)} %get-tuple-element.19) | data formatting | bytes 8388608 | tf_op jit(solution)/shard_map/slice | solution.py:144
  206.3 5.6 fusion.4
  219.0 5.4 fusion.71
  239.8 5.0 convolution_convert_fusion.1
  244.8 12.7 %fusion.9 = bf16[16,8,128,128]{2,3,1,0:T(8,128)(2,1)} fusion(f32[16,8,128,128]{3,2,1,0:T(8,128)} %get-tuple-element.29, f32[16]{0:T(128)S(1)} %convert_element_type.121, bf16[16,128,8,128]{1,3,2,0:T(8,128)(2,1)} %bitcast.258, bf16[16,128,8,128]{1,3,2,0:T(8,128)(2,1)} %bitcast.261), kind=kOutput, calls=%fused_computation.20 | convolution fusion | flops 562036736 | bytes 20971584 | tf_op jit(solution)/shard_map/pqhd,pkhd->phqk/dot_general | solution.py:50
  257.4 6.7 %copy.315 = bf16[16,128,1024]{2,1,0:T(8,128)(2,1)} copy(bf16[16,128,1024]{1,2,0:T(8,128)(2,1)} %bitcast.263) | data formatting | bytes 8388608 | tf_op jit(solution)/shard_map/reshape | solution.py:73
  264.1 8.4 %convolution_convert_fusion.2 = bf16[16,8,128,128]{2,3,1,0:T(8,128)(2,1)} fusion(bf16[16,8,128,128]{2,3,1,0:T(8,128)(2,1)} %fusion.9, bf16[16,128,8,128]{1,3,2,0:T(8,128)(2,1)} %bitcast.256), kind=kOutput, calls=%fused_computation.26 | convolution fusion | flops 538968064 | bytes 12582912 | tf_op jit(solution)/shard_map/phqk,pqhd->pkhd/dot_general | solution.py:66
  272.5 6.4 %copy.314 = bf16[16,128,1024]{2,1,0:T(8,128)(2,1)} copy(bf16[16,128,1024]{1,2,0:T(8,128)(2,1)} %bitcast.265) | data formatting | bytes 8388608 | tf_op jit(solution)/shard_map/reshape | solution.py:72
  279.0 8.3 %pad_maximum_fusion = bf16[16,128,2048]{2,1,0:T(8,128)(2,1)} fusion(bf16[16,128,1024]{2,1,0:T(8,128)(2,1)} %copy.315, bf16[16,128,1024]{2,1,0:T(8,128)(2,1)} %copy.314), kind=kLoop, calls=%fused_computation.5 | loop fusion | flops 16777216 | bytes 16777216 | tf_op jit(solution)/shard_map/concatenate | solution.py:193
  287.3 11.3 %copy.339 = bf16[2,8,128,2048]{3,1,2,0:T(8,128)(2,1)} copy(bf16[2,8,128,2048]{3,2,1,0:T(8,128)(2,1)} %bitcast.252) | data formatting | bytes 16777216
  298.6 11.4 %convolution_convert_fusion = bf16[24,262144]{1,0:T(8,128)(2,1)} fusion(bf16[16,262144]{1,0:T(8,128)(2,1)} %bitcast.249, s32[16]{0:T(128)S(1)} %bitcast.300), kind=kOutput, calls=%fused_computation.3 | convolution fusion | flops 207618432 | bytes 20971584 | tf_op jit(solution)/shard_map/dot_general | solution.py:194
  309.9 14.7 %copy.340 = bf16[3,8,128,2048]{3,2,1,0:T(8,128)(2,1)} copy(bf16[3,8,128,2048]{3,1,2,0:T(8,128)(2,1)} %bitcast.247) | data formatting | bytes 25165824
  324.6 17.8 %all-to-all-start.1 = ((bf16[8,3,128,2048]{3,2,1,0:T(8,128)(2,1)}), bf16[8,3,128,2048]{3,2,1,0:T(8,128)(2,1)}, u32[]{:S(2)}, u32[]{:S(2)}) async-start(bf16[8,3,128,2048]{3,2,1,0:T(8,128)(2,1)} %bitcast.250), calls=%async_computation.1 | async-start | bytes 25165824 | tf_op jit(solution)/shard_map/all_to_all | solution.py:198
  351.6 4.9 fusion.34
  395.8 147.2 %psum.7 = f32[1024]{0:T(1024)} all-reduce(f32[1024]{0:T(1024)S(1)} %get-tuple-element.7), channel_id=1, replica_groups=mesh['seq'=8,'dp'=4] {'seq','dp'}, use_global_device_ids=true, to_apply=%region_11.12 | all-reduce | flops 1024 | bytes 8192 | tf_op jit(solution)/shard_map/psum | solution.py:173
  552.9 11.7 %copy.341 = bf16[3,8,128,2048]{3,1,2,0:T(8,128)(2,1)S(1)} copy(bf16[3,8,128,2048]{3,2,1,0:T(8,128)(2,1)} %bitcast.95) | data formatting | bytes 25165824
  572.3 5.4 copy.316
  (157 shorter events, 142.2 us)
Async XLA Ops:
  7.2 43.2 %copy-start = (bf16[1024,1024]{1,0:T(8,128)(2,1)S(1)}, bf16[1024,1024]{1,0:T(8,128)(2,1)}, u32[]{:S(2)}) copy-start(bf16[1024,1024]{1,0:T(8,128)(2,1)} %param.17) | copy-start | bytes 6291460
  9.0 3.2 copy-start.30
  30.3 5.5 copy-start.11
  30.3 145.3 %all-to-all-start = ((bf16[8,3,128,2048]{3,2,1,0:T(8,128)(2,1)}), bf16[8,3,128,2048]{3,2,1,0:T(8,128)(2,1)}, u32[]{:S(2)}, u32[]{:S(2)}) async-start(bf16[8,3,128,2048]{3,2,1,0:T(8,128)(2,1)} %broadcast_select_fusion), calls=%async_computation | async-start | bytes 25165824 | tf_op jit(solution)/shard_map/all_to_all | solution.py:134
  35.8 5.0 copy-start.32
  37.6 25.2 %collective-permute-start = (bf16[128,2048]{1,0:T(8,128)(2,1)}, bf16[128,2048]{1,0:T(8,128)(2,1)}, u32[]{:S(2)}, u32[]{:S(2)}) collective-permute-start(bf16[128,2048]{1,0:T(8,128)(2,1)} %fusion.48), channel_id=1, source_target_pairs={{0,4},{4,8},{8,12},{12,16},{16,20},{20,24},{24,28},{1,5},{5,9},{9,... | collective-permute-start | bytes 1572872 | tf_op jit(solution)/shard_map/ppermute | solution.py:16
  45.3 2.8 copy-start.14
  50.4 2.6 copy-start.1
  58.4 4.4 copy-start.19
  203.8 2.5 copy-start.9
  206.0 5.9 copy-start.7
  206.3 5.6 copy-start.10
  224.6 2.9 copy-start.29
  227.5 4.6 copy-start.4
  227.5 4.6 copy-start.12
  237.3 2.5 copy-start.6
  239.4 5.3 copy-start.8
  324.6 228.2 %all-to-all-start.1 = ((bf16[8,3,128,2048]{3,2,1,0:T(8,128)(2,1)}), bf16[8,3,128,2048]{3,2,1,0:T(8,128)(2,1)}, u32[]{:S(2)}, u32[]{:S(2)}) async-start(bf16[8,3,128,2048]{3,2,1,0:T(8,128)(2,1)} %bitcast.250), calls=%async_computation.1 | async-start | bytes 25165824 | tf_op jit(solution)/shard_map/all_to_all | solution.py:198
  342.4 244.6 %reduce-scatter.2.cloned.1.call-start = ((), (), s32[]{:S(2)}) async-start(), calls=%async_computation.3 | async-start | bytes 4325376 | tf_op jit(solution)/shard_map/reduce_scatter | solution.py:163
  368.3 2.3 copy-start.22
  368.3 2.6 copy-start.25
  384.6 193.1 %collective-permute-start.1 = (bf16[128,2048]{0,1:T(8,128)(2,1)}, bf16[128,2048]{0,1:T(8,128)(2,1)}, u32[]{:S(2)}, u32[]{:S(2)}) collective-permute-start(bf16[128,2048]{0,1:T(8,128)(2,1)} %slice_bitcast_fusion), channel_id=1, source_target_pairs={{4,0},{8,4},{12,8},{16,12},{20,16},{24,20},{28,24},{5,1},{9,5},{13... | collective-permute-start | bytes 1572872 | tf_op jit(solution)/shard_map/ppermute | solution.py:16
  543.0 3.1 copy-start.17
  543.0 3.1 copy-start.18
  (14 other events, 23.7 us)
Sparse Core Ops, SparseCore 0:
  356.6 152.8 reduce-scatter.1
where the time goes:
time: 606 us; the launch traced here: 594 us
  local copies, waits for them, and re-layouts  159 us (26%)
  blocking collectives  147 us (24%)
  waiting for transfers between devices  103 us (17%)
  matrix products  89.9 us (15%)
  other arithmetic  52.6 us (9%)
  starting transfers between devices  27.9 us (5%)
  between operations  14.8 us (2%)
    psum x1, blocking collectives, body(): grad_gain = lax.psum(jnp.sum(scaled * normed, axis=0), ('seq', 'dp'))  147 us
    all_to_all x1, waiting for transfers between devices, body(): lax.all_to_all(send_both.reshape(seq_count, capacity, BLK, 2 * width), 's...  103 us
    unnamed x75, local copies, waits for them, and re-layouts  57.6 us
    all_to_all x1, starting transfers between devices, body(): lax.all_to_all(send_back.reshape(seq_count, capacity, BLK, 2 * width), 's...  17.8 us
    dot_general x3, matrix products, pair_backward(): jnp.einsum('pqhd,pkhd->phqk', grad_heads, to_heads(value_part), preferred...  17.5 us
    slice x2, local copies, waits for them, and re-layouts, body(): far_keys = far_both[:, :, :width]  12.5 us
  transfers between devices with their start and end apart: 5, of which 1 were waited for; matrix products, arithmetic and copies ran while one was open for 21% of the time, Pallas kernels for 0%

commit v1 on v0

--- a/solution.py
+++ b/solution.py
@@ -170,7 +170,7 @@
     )
     grad_gate = as_bf16(grad_mixed * normed * norm_gain)
     scaled = grad_mixed * gate_vals
-    grad_gain = lax.psum(jnp.sum(scaled * normed, axis=0), ("seq", "dp"))
+    grad_gain = lax.psum(lax.psum(jnp.sum(scaled * normed, axis=0), "dp"), "seq")
     grad_hat = scaled * norm_gain
     grad_attn = inv_std * (
         grad_hat

time: 606 us -> 578 us (0.954)
  the two profiles are of different devices: /device:TPU:0 before, /device:TPU:28 now
where the time goes in v1:
time: 578 us; the launch traced here: 566 us
  local copies, waits for them, and re-layouts  159 us (28%)
  waiting for transfers between devices  117 us (20%)
  blocking collectives  117 us (20%)
  matrix products  89.9 us (16%)
  other arithmetic  52.5 us (9%)
  starting transfers between devices  15.5 us (3%)
  between operations  14.8 us (3%)
    ppermute x2, waiting for transfers between devices, from_behind(): return lax.ppermute(value, axis, pairs)  117 us
    psum x1, blocking collectives, body(): lax.psum(lax.psum(jnp.sum(scaled * normed, axis=0), 'dp'), 'seq')  109 us
    unnamed x75, local copies, waits for them, and re-layouts  57.7 us
    dot_general x3, matrix products, pair_backward(): jnp.einsum('pqhd,pkhd->phqk', grad_heads, to_heads(value_part), preferred...  17.6 us
    slice x2, local copies, waits for them, and re-layouts, body(): far_keys = far_both[:, :, :width]  12.4 us
    dot_general x3, matrix products, pair_backward(): jnp.einsum('phqk,pqhd->pkhd', grad_scores, to_heads(query_part), preferre...  12 us
  transfers between devices with their start and end apart: 5, of which 1 were waited for; matrix products, arithmetic and copies ran while one was open for 22% of the time, Pallas kernels for 0%

profile of v1, /device:TPU:28, one launch (start us, length us, event | category | flops | bytes accessed | tf_op | source)
XLA Modules:
  0.0 566.2 jit_solution(10489334604977552154)
XLA Ops:
  12.2 7.5 %gather_fusion = bf16[24,128,2048]{2,1,0:T(8,128)(2,1)} fusion(bf16[4,128,2048]{2,1,0:T(8,128)(2,1)} %pad_maximum_fusion.1, s32[1024]{0:T(1024)S(1)} %pad_clamp_fusion.2), kind=kCustom, calls=%fused_computation | custom fusion | bytes 25165920 | tf_op jit(solution)/shard_map/gather | solution.py:132
  19.7 10.6 %broadcast_select_fusion = bf16[8,3,128,2048]{3,2,1,0:T(8,128)(2,1)} fusion(bf16[8,3,128,2048]{3,2,1,0:T(8,128)(2,1)} %bitcast.251, pred[8,3]{1,0:T(8,128)(4,1)S(1)} %copy.282), kind=kLoop, calls=%fused_computation.4 | loop fusion | flops 6291456 | bytes 25165848 | tf_op jit(solution)/shard_map/jit(_where)/select_n | solution.py:131
  30.3 6.0 %all-to-all-start = ((bf16[8,3,128,2048]{3,2,1,0:T(8,128)(2,1)}), bf16[8,3,128,2048]{3,2,1,0:T(8,128)(2,1)}, u32[]{:S(2)}, u32[]{:S(2)}) async-start(bf16[8,3,128,2048]{3,2,1,0:T(8,128)(2,1)} %broadcast_select_fusion), calls=%async_computation | async-start | bytes 25165824 | tf_op jit(solution)/shard_map/all_to_all | solution.py:134
  62.2 117.4 %collective-permute-done = bf16[128,2048]{1,0:T(8,128)(2,1)} collective-permute-done((bf16[128,2048]{1,0:T(8,128)(2,1)}, bf16[128,2048]{1,0:T(8,128)(2,1)}, u32[]{:S(2)}, u32[]{:S(2)}) %collective-permute-start) | collective-permute-done | bytes 524320 | tf_op jit(solution)/shard_map/ppermute | solution.py:16
  189.7 9.5 %gather_fusion.1 = bf16[16,128,2048]{2,1,0:T(8,128)(2,1)} fusion(bf16[24,128,2048]{2,1,0:T(8,128)(2,1)} %bitcast.11, s32[1024]{0:T(1024)S(1)} %pad_clamp_fusion.1), kind=kCustom, calls=%fused_computation.1 | custom fusion | bytes 16777280 | tf_op jit(solution)/shard_map/gather | solution.py:142
  199.2 6.0 %fusion.73 = (bf16[16,128,1024]{2,1,0:T(8,128)(2,1)}, bf16[16,128,1024]{2,1,0:T(8,128)(2,1)}) fusion(bf16[16,128,2048]{2,1,0:T(8,128)(2,1)} %gather_fusion.1), kind=kLoop, calls=%fused_computation.143 | loop fusion | bytes 16777216 | tf_op jit(solution)/shard_map/slice | solution.py:143
  205.2 6.4 %copy.285 = bf16[16,128,1024]{1,2,0:T(8,128)(2,1)} copy(bf16[16,128,1024]{2,1,0:T(8,128)(2,1)} %get-tuple-element.18) | data formatting | bytes 8388608 | tf_op jit(solution)/shard_map/slice | solution.py:143
  211.6 6.3 %copy.284 = bf16[16,128,1024]{1,2,0:T(8,128)(2,1)} copy(bf16[16,128,1024]{2,1,0:T(8,128)(2,1)} %get-tuple-element.19) | data formatting | bytes 8388608 | tf_op jit(solution)/shard_map/slice | solution.py:144
  220.4 5.6 fusion.4
  233.0 5.4 fusion.71
  253.8 5.0 convolution_convert_fusion.1
  258.8 12.7 %fusion.9 = bf16[16,8,128,128]{2,3,1,0:T(8,128)(2,1)} fusion(f32[16,8,128,128]{3,2,1,0:T(8,128)} %get-tuple-element.29, f32[16]{0:T(128)S(1)} %convert_element_type.121, bf16[16,128,8,128]{1,3,2,0:T(8,128)(2,1)} %bitcast.258, bf16[16,128,8,128]{1,3,2,0:T(8,128)(2,1)} %bitcast.261), kind=kOutput, calls=%fused_computation.20 | convolution fusion | flops 562036736 | bytes 20971584 | tf_op jit(solution)/shard_map/pqhd,pkhd->phqk/dot_general | solution.py:50
  271.5 6.7 %copy.315 = bf16[16,128,1024]{2,1,0:T(8,128)(2,1)} copy(bf16[16,128,1024]{1,2,0:T(8,128)(2,1)} %bitcast.263) | data formatting | bytes 8388608 | tf_op jit(solution)/shard_map/reshape | solution.py:73
  278.1 8.4 %convolution_convert_fusion.2 = bf16[16,8,128,128]{2,3,1,0:T(8,128)(2,1)} fusion(bf16[16,8,128,128]{2,3,1,0:T(8,128)(2,1)} %fusion.9, bf16[16,128,8,128]{1,3,2,0:T(8,128)(2,1)} %bitcast.256), kind=kOutput, calls=%fused_computation.26 | convolution fusion | flops 538968064 | bytes 12582912 | tf_op jit(solution)/shard_map/phqk,pqhd->pkhd/dot_general | solution.py:66
  286.6 6.4 %copy.314 = bf16[16,128,1024]{2,1,0:T(8,128)(2,1)} copy(bf16[16,128,1024]{1,2,0:T(8,128)(2,1)} %bitcast.265) | data formatting | bytes 8388608 | tf_op jit(solution)/shard_map/reshape | solution.py:72
  293.0 8.3 %pad_maximum_fusion = bf16[16,128,2048]{2,1,0:T(8,128)(2,1)} fusion(bf16[16,128,1024]{2,1,0:T(8,128)(2,1)} %copy.315, bf16[16,128,1024]{2,1,0:T(8,128)(2,1)} %copy.314), kind=kLoop, calls=%fused_computation.5 | loop fusion | flops 16777216 | bytes 16777216 | tf_op jit(solution)/shard_map/concatenate | solution.py:193
  301.3 11.3 %copy.339 = bf16[2,8,128,2048]{3,1,2,0:T(8,128)(2,1)} copy(bf16[2,8,128,2048]{3,2,1,0:T(8,128)(2,1)} %bitcast.252) | data formatting | bytes 16777216
  312.5 11.4 %convolution_convert_fusion = bf16[24,262144]{1,0:T(8,128)(2,1)} fusion(bf16[16,262144]{1,0:T(8,128)(2,1)} %bitcast.249, s32[16]{0:T(128)S(1)} %bitcast.300), kind=kOutput, calls=%fused_computation.3 | convolution fusion | flops 207618432 | bytes 20971584 | tf_op jit(solution)/shard_map/dot_general | solution.py:194
  323.9 14.7 %copy.340 = bf16[3,8,128,2048]{3,2,1,0:T(8,128)(2,1)} copy(bf16[3,8,128,2048]{3,1,2,0:T(8,128)(2,1)} %bitcast.247) | data formatting | bytes 25165824
  338.6 5.3 all-to-all-start.1
  398.0 8.3 %psum.14 = f32[1024]{0:T(1024)S(1)} all-reduce(f32[1024]{0:T(1024)S(1)} %get-tuple-element.7), channel_id=1, replica_groups=mesh['seq'=8,'dp'=4] {'dp'}, use_global_device_ids=true, to_apply=%region_11.12 | all-reduce | flops 1024 | bytes 8192 | tf_op jit(solution)/shard_map/psum | solution.py:173
  406.3 108.8 %psum.15 = f32[1024]{0:T(1024)} all-reduce(f32[1024]{0:T(1024)S(1)} %psum.14), channel_id=1, replica_groups=mesh['seq'=8,'dp'=4] {'seq'}, use_global_device_ids=true, to_apply=%region_12.13 | all-reduce | flops 1024 | bytes 8192 | tf_op jit(solution)/shard_map/psum | solution.py:173
  524.9 11.7 %copy.341 = bf16[3,8,128,2048]{3,1,2,0:T(8,128)(2,1)S(1)} copy(bf16[3,8,128,2048]{3,2,1,0:T(8,128)(2,1)} %bitcast.95) | data formatting | bytes 25165824
  544.4 5.3 copy.316
  (158 shorter events, 146.6 us)
Async XLA Ops:
  7.2 42.6 %copy-start = (bf16[1024,1024]{1,0:T(8,128)(2,1)S(1)}, bf16[1024,1024]{1,0:T(8,128)(2,1)}, u32[]{:S(2)}) copy-start(bf16[1024,1024]{1,0:T(8,128)(2,1)} %param.17) | copy-start | bytes 6291460
  9.0 3.2 copy-start.30
  30.3 6.0 %copy-start.11 = (bf16[1,512,1024]{2,1,0:T(8,128)(2,1)S(1)}, bf16[1,512,1024]{2,1,0:T(8,128)(2,1)}, u32[]{:S(2)}) copy-start(bf16[1,512,1024]{2,1,0:T(8,128)(2,1)} %param.10) | copy-start | bytes 3145732
  30.3 159.4 %all-to-all-start = ((bf16[8,3,128,2048]{3,2,1,0:T(8,128)(2,1)}), bf16[8,3,128,2048]{3,2,1,0:T(8,128)(2,1)}, u32[]{:S(2)}, u32[]{:S(2)}) async-start(bf16[8,3,128,2048]{3,2,1,0:T(8,128)(2,1)} %broadcast_select_fusion), calls=%async_computation | async-start | bytes 25165824 | tf_op jit(solution)/shard_map/all_to_all | solution.py:134
  36.3 3.9 copy-start.32
  38.1 141.4 %collective-permute-start = (bf16[128,2048]{1,0:T(8,128)(2,1)}, bf16[128,2048]{1,0:T(8,128)(2,1)}, u32[]{:S(2)}, u32[]{:S(2)}) collective-permute-start(bf16[128,2048]{1,0:T(8,128)(2,1)} %fusion.48), channel_id=1, source_target_pairs={{0,4},{4,8},{8,12},{12,16},{16,20},{20,24},{24,28},{1,5},{5,9},{9,... | collective-permute-start | bytes 1572872 | tf_op jit(solution)/shard_map/ppermute | solution.py:16
  44.7 2.8 copy-start.14
  49.8 2.6 copy-start.1
  57.8 121.7 %copy-start.19 = (bf16[3,128,2048]{2,1,0:T(8,128)(2,1)S(1)}, bf16[3,128,2048]{2,1,0:T(8,128)(2,1)}, u32[]{:S(2)}) copy-start(bf16[3,128,2048]{2,1,0:T(8,128)(2,1)} %fusion.29) | copy-start | bytes 4718596
  217.9 2.5 copy-start.9
  220.1 5.9 %copy-start.7 = (bf16[4,4,128,1024]{2,3,1,0:T(8,128)(2,1)}, bf16[4,4,128,1024]{2,3,1,0:T(8,128)(2,1)S(1)}, u32[]{:S(2)}) copy-start(bf16[4,4,128,1024]{2,3,1,0:T(8,128)(2,1)S(1)} %broadcast_in_dim.78) | copy-start | bytes 12582916
  220.4 5.6 copy-start.10
  238.6 2.9 copy-start.29
  241.6 4.6 copy-start.4
  241.6 4.6 copy-start.12
  251.3 2.5 copy-start.6
  253.5 5.3 copy-start.8
  338.6 186.3 %all-to-all-start.1 = ((bf16[8,3,128,2048]{3,2,1,0:T(8,128)(2,1)}), bf16[8,3,128,2048]{3,2,1,0:T(8,128)(2,1)}, u32[]{:S(2)}, u32[]{:S(2)}) async-start(bf16[8,3,128,2048]{3,2,1,0:T(8,128)(2,1)} %bitcast.250), calls=%async_computation.1 | async-start | bytes 25165824 | tf_op jit(solution)/shard_map/all_to_all | solution.py:198
  343.9 215.1 %reduce-scatter.2.cloned.1.call-start = ((), (), s32[]{:S(2)}) async-start(), calls=%async_computation.3 | async-start | bytes 4325376 | tf_op jit(solution)/shard_map/reduce_scatter | solution.py:163
  369.9 2.4 copy-start.22
  369.9 2.6 copy-start.25
  386.2 163.5 %collective-permute-start.1 = (bf16[128,2048]{0,1:T(8,128)(2,1)}, bf16[128,2048]{0,1:T(8,128)(2,1)}, u32[]{:S(2)}, u32[]{:S(2)}) collective-permute-start(bf16[128,2048]{0,1:T(8,128)(2,1)} %slice_bitcast_fusion), channel_id=1, source_target_pairs={{4,0},{8,4},{12,8},{16,12},{20,16},{24,20},{28,24},{5,1},{9,5},{13... | collective-permute-start | bytes 1572872 | tf_op jit(solution)/shard_map/ppermute | solution.py:16
  515.1 3.1 copy-start.17
  515.1 3.1 copy-start.18
  (14 other events, 23.6 us)
Sparse Core Ops, SparseCore 0:
  358.1 142.3 reduce-scatter.1
